TPU v7x, 256 devices: a whole 4x4x8 slice. The times are simulated.
256 devices in a mesh: dp: 4 (over z_lo), sp: 64 (over x, z_hi, y, core).
Axes of the slice: x: 4, y: 4, z: 8 (z_hi: 2, z_lo: 4; z = z_hi * 4 + z_lo), core: 2. Of those that a mesh axis runs over, the one named last changes fastest.
Arguments:
- inputs: bfloat16 [4, 384, 768, 384], P('dp', 'sp'), may hold values from -6 to 6
- cotangent: bfloat16 [4, 384, 768, 384], P('dp', 'sp'), may hold values from -6 to 6
- masks: int32 [4, 256, 256, 384], P('dp', None, 'sp'), may hold values from 0 to 15
- w_first: bfloat16 [2, 4, 96, 96], replicated, may hold values from -0.4375 to 0.4375
- b_first: float32 [2, 384], replicated, may hold values from -4 to 4
- w_second: bfloat16 [2, 4, 96, 96], replicated, may hold values from -0.4375 to 0.4375
Outputs:
- grad_input: bfloat16 [4, 384, 768, 384], P('dp', 'sp')
- grad_w1: float32 [2, 4, 96, 96], replicated
- grad_b1: float32 [2, 384], replicated
- grad_w2: float32 [2, 4, 96, 96], replicated
- grad_b2: float32 [2, 384], replicated
All inputs are finite; a program needn't handle non-finite values.
Results may differ from a plain program's by a relative error of at most 0.0086.
Values may be sent and summed in bfloat16 or wider, within the bound.
A program may use at most 128 MiB of HBM per device.

v0:
```python
import math

import jax
import jax.numpy as jnp
from jax import lax
from jax.sharding import PartitionSpec as P


def lon_table(count, length):
    modes = jnp.arange(count, dtype=jnp.int32)
    points = jnp.arange(length, dtype=jnp.int32)
    phase = modes[:, None] * points[None, :] % length
    angle = 2.0 * math.pi / length * phase.astype(jnp.float32)
    return jnp.stack([jnp.cos(angle).astype(jnp.bfloat16), -jnp.sin(angle).astype(jnp.bfloat16)])


def lat_tables(keep, length):
    half_keep = keep // 2
    index = jnp.arange(keep, dtype=jnp.int32)
    modes = jnp.where(index < half_keep, index, index + (length - keep))
    points = jnp.arange(length, dtype=jnp.int32)
    phase = modes[:, None] * points[None, :] % length
    angle = 2.0 * math.pi / length * phase.astype(jnp.float32)
    cosine = jnp.cos(angle).astype(jnp.bfloat16)
    sine = jnp.sin(angle).astype(jnp.bfloat16)
    forward = jnp.stack([jnp.stack([cosine, sine], 1), jnp.stack([-sine, cosine], 1)])
    backward = jnp.stack([jnp.stack([cosine.T, -sine.T], 1), jnp.stack([sine.T, cosine.T], 1)])
    return (forward, backward)


def contract(form, left, right):
    return jnp.einsum(form, left, right, preferred_element_type=jnp.float32)


def complex_mul(real, imag, w_real, w_imag):
    form = "jkbi,bio->jkbo"
    return (
        contract(form, real, w_real) - contract(form, imag, w_imag),
        contract(form, real, w_imag) + contract(form, imag, w_real),
    )


def complex_adjoint(real, imag, w_real, w_imag):
    form = "jkbo,bio->jkbi"
    return (
        contract(form, real, w_real) + contract(form, imag, w_imag),
        contract(form, imag, w_real) - contract(form, real, w_imag),
    )


def weight_grad(left_re, left_im, right_re, right_im):
    form = "jkbi,jkbo->bio"
    return jnp.stack(
        [
            contract(form, left_re, right_re) + contract(form, left_im, right_im),
            contract(form, left_re, right_im) - contract(form, left_im, right_re),
        ]
    )


def bias_grad(real, imag, channels):
    return jnp.stack(
        [
            jnp.sum(real.astype(jnp.float32), axis=(0, 1)),
            jnp.sum(imag.astype(jnp.float32), axis=(0, 1)),
        ]
    ).reshape(2, channels)


def local(inputs, cotangent, masks, w_first, b_first, w_second):
    rows_dev = inputs.shape[1]
    lon_len = inputs.shape[2]
    channels = inputs.shape[3]
    width_sp = lax.axis_size("sp")
    members = lax.axis_size("dp")
    keep_lat = masks.shape[1]
    kx_dev = masks.shape[2]
    keep_lon = kx_dev * width_sp
    lat_len = rows_dev * width_sp
    blocks_count = w_first.shape[1]
    block_width = w_first.shape[2]
    blocks = (keep_lat, kx_dev, blocks_count, block_width)
    lon_tab = lon_table(keep_lon, lon_len)
    lat_fwd, lat_back = lat_tables(keep_lat, lat_len)
    factor = 1.0 / math.sqrt(lat_len * lon_len)
    global_modes = lax.axis_index("sp") * kx_dev + jnp.arange(kx_dev, dtype=jnp.int32)
    mode_weight = jnp.where(global_modes == 0, 1.0, 2.0).astype(jnp.float32)

    def row_spectrum(field):
        return contract("pkw,hwc->pkhc", lon_tab, field[0]).astype(jnp.bfloat16)

    y_input = row_spectrum(inputs)
    y_cotan = row_spectrum(cotangent)
    spectrum = (
        contract(
            "qjph,pkhc->qjkc",
            lat_fwd,
            lax.all_to_all(y_input, "sp", split_axis=1, concat_axis=2, tiled=True),
        )
        * factor
    ).astype(jnp.bfloat16)
    d_out = (
        contract(
            "qjph,pkhc->qjkc",
            lat_fwd,
            lax.all_to_all(y_cotan, "sp", split_axis=1, concat_axis=2, tiled=True),
        )
        * factor
        * mode_weight[None, None, :, None]
    ).astype(jnp.bfloat16)
    packed = masks[0]
    relu_re = (packed % 2).astype(jnp.float32).reshape(blocks)
    relu_im = (packed // 2 % 2).astype(jnp.float32).reshape(blocks)
    shrink_re = (packed // 4 % 2).astype(jnp.float32).reshape(blocks)
    shrink_im = (packed // 8 % 2).astype(jnp.float32).reshape(blocks)
    bias_re = b_first[0].reshape(blocks_count, block_width)
    bias_im = b_first[1].reshape(blocks_count, block_width)
    spec_re = spectrum[0].reshape(blocks)
    spec_im = spectrum[1].reshape(blocks)
    pre_re, pre_im = complex_mul(spec_re, spec_im, w_first[0], w_first[1])
    hidden_re = ((pre_re + bias_re) * relu_re).astype(jnp.bfloat16)
    hidden_im = ((pre_im + bias_im) * relu_im).astype(jnp.bfloat16)
    dtwo_re = (d_out[0].reshape(blocks).astype(jnp.float32) * shrink_re).astype(jnp.bfloat16)
    dtwo_im = (d_out[1].reshape(blocks).astype(jnp.float32) * shrink_im).astype(jnp.bfloat16)
    second_terms = (
        weight_grad(hidden_re, hidden_im, dtwo_re, dtwo_im),
        bias_grad(dtwo_re, dtwo_im, channels),
    )
    back_re, back_im = complex_adjoint(dtwo_re, dtwo_im, w_second[0], w_second[1])
    done_re = (back_re * relu_re).astype(jnp.bfloat16)
    done_im = (back_im * relu_im).astype(jnp.bfloat16)
    first_terms = (
        weight_grad(spec_re, spec_im, done_re, done_im),
        bias_grad(done_re, done_im, channels),
    )
    dspec_re, dspec_im = complex_adjoint(done_re, done_im, w_first[0], w_first[1])
    d_spec = (
        jnp.stack([dspec_re, dspec_im]).reshape(2, keep_lat, kx_dev, channels).astype(jnp.bfloat16)
    )
    columns = contract("phqj,qjkc->phkc", lat_back, d_spec).astype(jnp.bfloat16)
    image_rows = lax.all_to_all(columns, "sp", split_axis=1, concat_axis=2, tiled=True)
    grad_field = (
        cotangent[0].astype(jnp.float32) + factor * contract("pkw,phkc->hwc", lon_tab, image_rows)
    ).astype(jnp.bfloat16)
    grad_w1, grad_b1, grad_w2, grad_b2 = lax.psum(
        (first_terms[0], first_terms[1], second_terms[0], second_terms[1]), ("dp", "sp")
    )
    norm = 1.0 / math.sqrt(members * keep_lat * keep_lon)
    return (grad_field[None], grad_w1 * norm, grad_b1 * norm, grad_w2 * norm, grad_b2 * norm)


def solution(mesh):
    placed = (
        P("dp", "sp", None, None),
        P("dp", "sp", None, None),
        P("dp", None, "sp", None),
        P(),
        P(),
        P(),
    )
    return jax.shard_map(
        local,
        mesh=mesh,
        in_specs=placed,
        out_specs=(P("dp", "sp", None, None), P(), P(), P(), P()),
        check_vma=False,
    )
```

profile of v0, /device:TPU:1, one launch (start us, length us, event | category | flops | bytes accessed | tf_op | source)
XLA Modules:
  0.0 482.2 jit_solution(10230906674423413052)
XLA Ops:
  7.2 3.1 cosine_convert_fusion
  10.3 3.1 fusion.93
  14.1 4.0 fusion.18
  18.2 3.8 copy.122
  22.0 16.5 %all-to-all-start = ((bf16[2,256,6,384]{3,0,2,1:T(2,128)(2,1)}), bf16[2,256,6,384]{3,0,2,1:T(2,128)(2,1)}, u32[]{:S(2)}, u32[]{:S(2)}) async-start(bf16[2,256,6,384]{3,0,2,1:T(2,128)(2,1)} %copy.122), calls=%async_computation | async-start | bytes 4718592 | tf_op jit(solution)/shard_map/all_to_all | solution.py:106
  38.5 3.1 fusion.15
  41.6 3.9 copy.142
  45.5 1.7 fusion.129
  47.2 1.8 sine_convert_fusion.1
  49.2 45.0 %all-to-all-done = bf16[2,256,6,384]{3,0,2,1:T(2,128)(2,1)} async-done(((bf16[2,256,6,384]{3,0,2,1:T(2,128)(2,1)}), bf16[2,256,6,384]{3,0,2,1:T(2,128)(2,1)}, u32[]{:S(2)}, u32[]{:S(2)}) %all-to-all-start) | async-done | bytes 2359328 | tf_op jit(solution)/shard_map/all_to_all | solution.py:106
  94.2 5.4 %all-to-all-start.2 = ((bf16[2,256,6,384]{3,0,2,1:T(2,128)(2,1)}), bf16[2,256,6,384]{3,0,2,1:T(2,128)(2,1)}, u32[]{:S(2)}, u32[]{:S(2)}) async-start(bf16[2,256,6,384]{3,0,2,1:T(2,128)(2,1)} %copy.142), calls=%async_computation.2 | async-start | bytes 4718592 | tf_op jit(solution)/shard_map/all_to_all | solution.py:98
  99.7 6.1 %copy.120 = bf16[1,6,768,384]{2,3,1,0:T(8,128)(2,1)} copy(bf16[1,6,768,384]{3,2,1,0:T(8,128)(2,1)} %param.7) | data formatting | bytes 7077888 | tf_op args[1]
  105.8 1.7 copy.126
  108.2 1.5 fusion.128
  109.8 1.7 sine_convert_fusion.2
  111.5 0.9 maximum_bitcast_fusion.7
  112.4 2.6 copy.123
  115.0 1.4 fusion.7
  116.4 1.5 slice_convert_fusion.1
  118.1 3.1 copy.125
  121.1 1.6 copy.132
  122.7 4.7 fusion.29
  127.8 1.0 copy-done.5
  128.9 1.0 convert_reduce_fusion.3
  130.3 1.0 copy-done.6
  131.3 1.9 convert_reduce_fusion.2
  133.3 4.8 convert_reduce_fusion.1
  138.1 4.0 copy.143
  142.5 1.5 fusion.108
  144.4 1.2 copy.136
  145.6 1.8 fusion.59
  147.4 1.2 copy.137
  148.6 3.0 bitcast_convert_fusion
  151.6 3.3 copy.138
  154.9 13.0 %all-to-all-start.1 = ((bf16[2,384,4,384]{3,2,0,1:T(4,128)(2,1)}), bf16[2,384,4,384]{3,2,0,1:T(4,128)(2,1)}, u32[]{:S(2)}, u32[]{:S(2)}) async-start(bf16[2,384,4,384]{3,2,0,1:T(4,128)(2,1)} %copy.138), calls=%async_computation.1 | async-start | bytes 4718592 | tf_op jit(solution)/shard_map/all_to_all | solution.py:141
  168.2 3.1 fusion.6
  171.3 1.3 fusion.137
  172.6 1.4 copy.145
  174.0 2.3 copy.147
  176.8 1.0 copy-done.7
  177.9 1.8 fusion.50
  181.2 1.0 fusion.51
  186.1 99.0 %all-reduce = (f32[2,384]{1,0:T(2,128)S(1)}, f32[2,384]{1,0:T(2,128)S(1)}) all-reduce(f32[2,384]{1,0:T(2,128)S(1)} %pad_maximum_fusion.6, f32[2,384]{1,0:T(2,128)S(1)} %pad_maximum_fusion.7), channel_id=1, replica_groups=mesh['dp'=4,'sp'=64] {'dp','sp'}, use_global_device_ids=true, to_apply=%region_3.4 | all-reduce | flops 1536 | bytes 12288 | tf_op jit(solution)/shard_map/psum | solution.py:145
  285.6 172.8 %all-reduce.4.cloned.1.call-done = (f32[2,4,96,96]{3,2,1,0:T(8,128)}, f32[2,4,96,96]{3,2,1,0:T(8,128)}) async-done(((f32[2,4,96,96]{3,2,1,0:T(8,128)}, f32[2,4,96,96]{3,2,1,0:T(8,128)}), (f32[2,4,96,96]{3,2,1,0:T(8,128)}, f32[2,4,96,96]{3,2,1,0:T(8,128)})) %all-reduce.4.cloned.1.call-update) | async-done | bytes 589840 | tf_op jit(solution)/shard_map/psum | solution.py:145
  458.4 2.0 broadcast_multiply_fusion
  460.5 4.2 copy.140
  464.8 3.9 fusion.1
  468.7 6.1 %copy.163 = bf16[1,6,768,384]{3,2,1,0:T(8,128)(2,1)} copy(bf16[1,6,768,384]{2,3,1,0:T(8,128)(2,1)} %fusion.1) | data formatting | bytes 7077888
  (78 shorter events, 10.2 us)
Async XLA Ops:
  7.2 31.3 %copy-start = (bf16[1,6,768,384]{3,2,1,0:T(8,128)(2,1)S(1)}, bf16[1,6,768,384]{3,2,1,0:T(8,128)(2,1)}, u32[]{:S(2)}) copy-start(bf16[1,6,768,384]{3,2,1,0:T(8,128)(2,1)} %param.6) | copy-start | bytes 10616836
  10.2 3.1 copy-start.12
  13.4 0.8 copy-start.14
  22.0 72.2 %all-to-all-start = ((bf16[2,256,6,384]{3,0,2,1:T(2,128)(2,1)}), bf16[2,256,6,384]{3,0,2,1:T(2,128)(2,1)}, u32[]{:S(2)}, u32[]{:S(2)}) async-start(bf16[2,256,6,384]{3,0,2,1:T(2,128)(2,1)} %copy.122), calls=%async_computation | async-start | bytes 4718592 | tf_op jit(solution)/shard_map/all_to_all | solution.py:106
  49.2 65.8 %copy-start.16 = (bf16[1,256,2,384]{3,1,2,0:T(8,128)(2,1)}, bf16[1,256,2,384]{3,1,2,0:T(8,128)(2,1)S(1)}, u32[]{:S(2)}) copy-start(bf16[1,256,2,384]{3,1,2,0:T(8,128)(2,1)S(1)} %get-tuple-element.41) | copy-start | bytes 1179652
  49.2 65.8 %copy-start.18 = (bf16[1,256,2,384]{3,1,2,0:T(8,128)(2,1)}, bf16[1,256,2,384]{3,1,2,0:T(8,128)(2,1)S(1)}, u32[]{:S(2)}) copy-start(bf16[1,256,2,384]{3,1,2,0:T(8,128)(2,1)S(1)} %get-tuple-element.42) | copy-start | bytes 1179652
  49.2 50.4 %copy-start.21 = (f32[2,384]{1,0:T(2,128)S(1)}, f32[2,384]{1,0:T(2,128)}, u32[]{:S(2)}) copy-start(f32[2,384]{1,0:T(2,128)} %param.10) | copy-start | bytes 9220
  94.2 43.9 %all-to-all-start.2 = ((bf16[2,256,6,384]{3,0,2,1:T(2,128)(2,1)}), bf16[2,256,6,384]{3,0,2,1:T(2,128)(2,1)}, u32[]{:S(2)}, u32[]{:S(2)}) async-start(bf16[2,256,6,384]{3,0,2,1:T(2,128)(2,1)} %copy.142), calls=%async_computation.2 | async-start | bytes 4718592 | tf_op jit(solution)/shard_map/all_to_all | solution.py:98
  99.6 6.1 %copy-start.4 = (s32[1,256,4,384]{3,2,1,0:T(4,128)S(1)}, s32[1,256,4,384]{3,2,1,0:T(4,128)}, u32[]{:S(2)}) copy-start(s32[1,256,4,384]{3,2,1,0:T(4,128)} %param.8) | copy-start | bytes 4718596
  116.4 1.7 copy-start.8
  122.7 4.7 copy-start.20
  127.4 1.4 copy-start.5
  129.9 1.4 copy-start.6
  133.2 10.8 %copy-start.2 = (bf16[256,4,4,96]{0,3,1,2:T(8,128)(2,1)}, bf16[256,4,4,96]{0,3,1,2:T(8,128)(2,1)S(1)}, u32[]{:S(2)}) copy-start(bf16[256,4,4,96]{0,3,1,2:T(8,128)(2,1)S(1)} %get-tuple-element.48) | copy-start | bytes 2359300
  138.1 4.1 copy-start.10
  154.8 13.4 %copy-start.17 = (bf16[1,256,2,384]{3,1,2,0:T(8,128)(2,1)S(1)}, bf16[1,256,2,384]{3,1,2,0:T(8,128)(2,1)}, u32[]{:S(2)}) copy-start(bf16[1,256,2,384]{3,1,2,0:T(8,128)(2,1)} %copy-done.16) | copy-start | bytes 1179652
  154.8 13.4 %copy-start.19 = (bf16[1,256,2,384]{3,1,2,0:T(8,128)(2,1)S(1)}, bf16[1,256,2,384]{3,1,2,0:T(8,128)(2,1)}, u32[]{:S(2)}) copy-start(bf16[1,256,2,384]{3,1,2,0:T(8,128)(2,1)} %copy-done.18) | copy-start | bytes 1179652
  154.9 305.6 %all-to-all-start.1 = ((bf16[2,384,4,384]{3,2,0,1:T(4,128)(2,1)}), bf16[2,384,4,384]{3,2,0,1:T(4,128)(2,1)}, u32[]{:S(2)}, u32[]{:S(2)}) async-start(bf16[2,384,4,384]{3,2,0,1:T(4,128)(2,1)} %copy.138), calls=%async_computation.1 | async-start | bytes 4718592 | tf_op jit(solution)/shard_map/all_to_all | solution.py:141
  167.9 290.5 %all-reduce.4.cloned.1.call-start = ((), (), s32[]{:S(2)}) async-start(), calls=%async_computation.3 | async-start | bytes 1572864 | tf_op jit(solution)/shard_map/psum | solution.py:145
  176.3 1.4 copy-start.7
  176.3 1.6 copy-start.11
  180.5 0.7 copy-start.22
  182.6 1.2 copy-start.3
  460.5 4.3 copy-start.9
  460.5 4.3 copy-start.13
  460.5 4.3 copy-start.15
  468.7 6.1 %copy-start.1 = (bf16[1,6,768,384]{3,2,1,0:T(8,128)(2,1)S(1)}, bf16[1,6,768,384]{3,2,1,0:T(8,128)(2,1)}, u32[]{:S(2)}) copy-start(bf16[1,6,768,384]{3,2,1,0:T(8,128)(2,1)} %param.6) | copy-start | bytes 10616836
Sparse Core Ops, SparseCore 0:
  186.1 272.2 all-reduce.3
where the time goes:
time: 490 us; the launch traced here: 482 us
  waiting for transfers between devices  218 us (44%)
  blocking collectives  99 us (20%)
  local copies, waits for them, and re-layouts  53.3 us (11%)
  starting transfers between devices  35.3 us (7%)
  matrix products  32.6 us (7%)
  other arithmetic  29.1 us (6%)
  between operations  15 us (3%)
    psum x1, waiting for transfers between devices, local(): lax.psum((first_terms[0], first_terms[1], second_terms[0], second_terms[1...  173 us
    psum x1, blocking collectives, local(): lax.psum((first_terms[0], first_terms[1], second_terms[0], second_terms[1...  99 us
    all_to_all x1, waiting for transfers between devices, local(): lax.all_to_all(y_cotan, 'sp', split_axis=1, concat_axis=2, tiled=True)  45 us
    dot_general x26, matrix products, contract(): return jnp.einsum(form, left, right, preferred_element_type=jnp.float32)  32.6 us
    unnamed x49, local copies, waits for them, and re-layouts  18.4 us
    all_to_all x1, starting transfers between devices, local(): lax.all_to_all(y_cotan, 'sp', split_axis=1, concat_axis=2, tiled=True)  16.5 us
    all_to_all x1, starting transfers between devices, local(): lax.all_to_all(columns, 'sp', split_axis=1, concat_axis=2, tiled=True)  13 us
  transfers between devices with their start and end apart: 4, of which 2 were waited for; matrix products, arithmetic and copies ran while one was open for 14% of the time, Pallas kernels for 0%

commit v1 on v0

v1 whole, which is shorter than its diff:
```python
import functools
import math

import jax
import jax.numpy as jnp
import ml_dtypes
import numpy as np
from jax import lax
from jax.experimental import pallas as pl
from jax.experimental.pallas import tpu as pltpu
from jax.sharding import PartitionSpec as P

MESH = pl.DeviceIdType.MESH
BF = jnp.bfloat16
F32 = jnp.float32
MIB = 2**20


def bf(array):
    return array.astype(np.float32).astype(ml_dtypes.bfloat16)


def lon_tables(count, length, devices):
    phase = (np.arange(count)[:, None] * np.arange(length)[None, :]) % length
    angle = (np.float32(2.0 * math.pi / length) * phase.astype(np.float32)).astype(np.float64)
    table = np.stack([np.cos(angle), -np.sin(angle)], 1).reshape(2 * count, length)
    return bf(table), bf(table.T)


def lat_tables(keep, length):
    index = np.arange(keep)
    modes = np.where(index < keep // 2, index, index + (length - keep))
    phase = (modes[:, None] * np.arange(length)[None, :]) % length
    angle = (np.float32(2.0 * math.pi / length) * phase.astype(np.float32)).astype(np.float64)
    cosine, sine = np.cos(angle), np.sin(angle)
    forward = np.stack([np.stack([cosine, sine], 2), np.stack([-sine, cosine], 2)])
    return bf(forward.reshape(2 * keep, 2 * length)), bf(forward.reshape(2 * keep, 2 * length).T)


def permutation(rows, modes):
    out = np.zeros((modes, rows, 2, rows, modes, 2), np.float32)
    for k in range(modes):
        for h in range(rows):
            for p in range(2):
                out[k, h, p, h, k, p] = 1.0
    size = modes * rows * 2
    out = out.reshape(size, size)
    return bf(out), bf(out.T)


def dot(left, right):
    return jnp.dot(left, right, preferred_element_type=F32)


def dot_tn(left, right):
    return lax.dot_general(left, right, (((0,), (0,)), ((), ())), preferred_element_type=F32)


def main_kernel(
    factor, norm,
    cot_hbm, inp_hbm, mask_hbm, lon_hbm, latf_hbm, latb_hbm, pf_ref, pb_ref, w1_ref, b1_ref, w2_ref,
    rows_out, grads_out,
    cot_v, inp_v, mask_v, lon_v, latf_v, latb_v,
    send_c, send_i, send_r, recv_c, recv_i, xt, spec, dtwo, done, hid, dsp, relu, shrink,
    m1, m2, m3, acc_a, acc_b, acc_s, fold, parts, gathered, plane, column, chunk, result,
    lsem, ssem, rsem,
):
    dp = lax.axis_index("dp")
    me = lax.axis_index("sp")
    x = me // 16
    z_hi = (me // 8) % 2
    low = me % 8
    p1 = x * 8 + low
    zi = z_hi * 4 + dp

    loads = [
        pltpu.make_async_copy(lon_hbm, lon_v, lsem.at[0]),
        pltpu.make_async_copy(cot_hbm.at[pl.ds(0, 2)], cot_v.at[pl.ds(0, 2)], lsem.at[1]),
        pltpu.make_async_copy(cot_hbm.at[pl.ds(2, 4)], cot_v.at[pl.ds(2, 4)], lsem.at[2]),
        pltpu.make_async_copy(inp_hbm, inp_v, lsem.at[3]),
        pltpu.make_async_copy(mask_hbm, mask_v, lsem.at[4]),
        pltpu.make_async_copy(latf_hbm, latf_v, lsem.at[5]),
        pltpu.make_async_copy(latb_hbm, latb_v, lsem.at[6]),
    ]
    for load in loads:
        load.start()

    barrier = pltpu.get_barrier_semaphore()

    def greet(o, carry):
        pl.semaphore_signal(barrier, inc=1, device_id=(dp, (me + o) % 64), device_id_type=MESH)
        return carry

    lax.fori_loop(1, 64, greet, 0)
    for o in range(1, 4):
        for zh in range(2):
            pl.semaphore_signal(
                barrier, inc=1, device_id=((dp + o) % 4, x * 16 + zh * 8 + low), device_id_type=MESH
            )

    def transform(field, send, hp):
        def part(m, carry):
            table = lon_v[pl.ds(pl.multiple_of(m * 128, 128), 128), :]
            first = dot(table, field[2 * hp]).reshape(16, 8, 384)
            second = dot(table, field[2 * hp + 1]).reshape(16, 8, 384)
            send[hp, pl.ds(m * 16, 16)] = jnp.concatenate([first, second], axis=1).astype(BF)
            return carry

        lax.fori_loop(0, 4, part, 0)

    def send_rows(send, recv, slot, hp):
        place = pl.ds(pl.multiple_of(me * 48 + hp * 16, 16), 16)
        recv[place, :] = send[hp, me]

        def one(o, carry):
            there = (me + o) % 64
            pltpu.make_async_remote_copy(
                src_ref=send.at[hp, there], dst_ref=recv.at[place], send_sem=ssem.at[slot],
                recv_sem=rsem.at[slot], device_id=(dp, there), device_id_type=MESH,
            ).start()
            return carry

        lax.fori_loop(1, 64, one, 0)

    loads[0].wait()
    loads[1].wait()
    transform(cot_v, send_c, 0)
    pl.semaphore_wait(barrier, 69)
    send_rows(send_c, recv_c, 0, 0)
    loads[2].wait()

    def cot_pair(hp, carry):
        transform(cot_v, send_c, hp)
        send_rows(send_c, recv_c, 0, hp)
        return carry

    lax.fori_loop(1, 3, cot_pair, 0)
    loads[3].wait()

    def inp_pair(hp, carry):
        transform(inp_v, send_i, hp)
        send_rows(send_i, recv_i, 1, hp)
        return carry

    lax.fori_loop(0, 3, inp_pair, 0)

    lane = lax.broadcasted_iota(jnp.int32, (96, 384), 1)
    row = lax.broadcasted_iota(jnp.int32, (96, 384), 0)
    for b in range(4):
        place = (lane == row + 96 * b).astype(BF)
        up = slice(96 * b, 96 * b + 96)
        dn = slice(384 + 96 * b, 384 + 96 * b + 96)
        w1r, w1i = w1_ref[0, b], w1_ref[1, b]
        w2r, w2i = w2_ref[0, b], w2_ref[1, b]
        real, imag = dot(w1r, place).astype(BF), dot(w1i, place).astype(BF)
        m1[up, 0:384] = real
        m1[up, 384:768] = imag
        m1[dn, 0:384] = -imag
        m1[dn, 384:768] = real
        for target, wr, wi in ((m2, w2r, w2i), (m3, w1r, w1i)):
            real, imag = dot_tn(wr, place).astype(BF), dot_tn(wi, place).astype(BF)
            target[up, 0:384] = real
            target[up, 384:768] = -imag
            target[dn, 0:384] = imag
            target[dn, 384:768] = real
    loads[4].wait()
    for kk in range(4):
        bits = mask_v[:, kk, :]
        here = slice(256 * kk, 256 * kk + 256)
        relu[here, 0:384] = (bits & 1).astype(F32).astype(BF)
        relu[here, 384:768] = ((bits >> 1) & 1).astype(F32).astype(BF)
        shrink[here, 0:384] = ((bits >> 2) & 1).astype(F32).astype(BF)
        shrink[here, 384:768] = ((bits >> 3) & 1).astype(F32).astype(BF)
    loads[5].wait()
    loads[6].wait()

    def arrived(recv, slot):
        view = recv.at[pl.ds(0, 63 * 48)]
        pltpu.make_async_remote_copy(
            src_ref=view, dst_ref=view, send_sem=ssem.at[slot], recv_sem=rsem.at[slot],
            device_id=(dp, me), device_id_type=MESH,
        ).wait_recv()

    def by_mode(recv):
        def block(g, carry):
            rows = dot(pf_ref[...], recv[pl.ds(pl.multiple_of(g * 256, 256), 256), :]).astype(BF)
            for kk in range(4):
                xt[kk, pl.ds(pl.multiple_of(g * 64, 64), 64), :] = rows[64 * kk:64 * kk + 64]
            return carry

        lax.fori_loop(0, 12, block, 0)

    def mode_rows(kk):
        return pl.ds(pl.multiple_of(kk * 256, 256), 256)

    arrived(recv_c, 0)
    by_mode(recv_c)

    def adjoint(kk, carry):
        here = mode_rows(kk)
        scale = jnp.where(me * 4 + kk == 0, factor, 2.0 * factor).astype(F32)
        for q in range(2):
            cols = slice(384 * q, 384 * q + 384)
            d_out = (dot(latf_v[256 * q:256 * q + 256, :], xt[kk]) * scale).astype(BF)
            dtwo[here, cols] = d_out * shrink[here, cols]
        back = dot(dtwo[here, :], m2[...]) * relu[here, :].astype(F32)
        done[here, :] = back.astype(BF)
        d_spec = dot(done[here, :], m3[...]).astype(BF)
        dsp[kk, 0:256, :] = d_spec[:, 0:384]
        dsp[kk, 256:512, :] = d_spec[:, 384:768]
        return carry

    lax.fori_loop(0, 4, adjoint, 0)

    own = pltpu.make_async_copy(
        send_r.at[pl.ds(pl.multiple_of(me * 48, 16), 48)],
        rows_out.at[pl.ds(pl.multiple_of(me * 48, 16), 48)], lsem.at[7],
    )

    def image_quarter(m):
        def block(b, carry):
            table = latb_v[pl.ds(pl.multiple_of(m * 192 + b * 64, 64), 64), :]
            image = jnp.concatenate([dot(table, dsp[kk]).astype(BF) for kk in range(4)], axis=0)
            place = pl.ds(pl.multiple_of(m * 768 + b * 256, 256), 256)
            send_r[place, :] = dot(pb_ref[...], image).astype(BF)
            return carry

        lax.fori_loop(0, 3, block, 0)

    for i in range(4):
        m = (x + i) % 4
        image_quarter(m)
        if i == 0:
            own.start()

        def one(o, carry):
            there = m * 16 + (me + o) % 16
            pltpu.make_async_remote_copy(
                src_ref=send_r.at[pl.ds(pl.multiple_of(there * 48, 16), 48)],
                dst_ref=rows_out.at[pl.ds(pl.multiple_of(me * 48, 16), 48)],
                send_sem=ssem.at[2], recv_sem=rsem.at[2],
                device_id=(dp, there), device_id_type=MESH,
            ).start()
            return carry

        lax.fori_loop(1 if i == 0 else 0, 16, one, 0)

    arrived(recv_i, 1)
    by_mode(recv_i)

    def layer(kk, carry):
        here = mode_rows(kk)
        for q in range(2):
            cols = slice(384 * q, 384 * q + 384)
            spec[here, cols] = (dot(latf_v[256 * q:256 * q + 256, :], xt[kk]) * factor).astype(BF)
        pre = dot(spec[here, :], m1[...])
        for q in range(2):
            cols = slice(384 * q, 384 * q + 384)
            kept = (pre[:, cols] + b1_ref[q:q + 1, :]) * relu[here, cols].astype(F32)
            hid[here, cols] = kept.astype(BF)
        return carry

    lax.fori_loop(0, 4, layer, 0)

    lanes = lax.broadcasted_iota(jnp.int32, (96, 384), 1) // 96
    for which, (left, right) in enumerate(((spec, done), (hid, dtwo))):
        acc_a[...] = jnp.zeros_like(acc_a)
        acc_b[...] = jnp.zeros_like(acc_b)
        acc_s[...] = jnp.zeros_like(acc_s)

        def add(kk, carry, left=left, right=right):
            here = mode_rows(kk)
            r = right[here, :]
            acc_a[...] += dot_tn(left[here, 0:384], r)
            acc_b[...] += dot_tn(left[here, 384:768], r)
            acc_s[...] += dot(jnp.ones((8, 256), BF), r)
            return carry

        lax.fori_loop(0, 4, add, 0)
        real = jnp.zeros((96, 384), F32)
        imag = jnp.zeros((96, 384), F32)
        for b in range(4):
            up = slice(96 * b, 96 * b + 96)
            real = jnp.where(lanes == b, acc_a[up, 0:384] + acc_b[up, 384:768], real)
            imag = jnp.where(lanes == b, acc_a[up, 384:768] - acc_b[up, 0:384], imag)
        fold[0:96, 0:384] = real
        fold[0:96, 384:768] = imag
        for r in range(12):
            for c in range(6):
                t = which * 72 + r * 6 + c
                parts[t // 5, t % 5] = fold[8 * r:8 * r + 8, 128 * c:128 * c + 128]
        for c in range(6):
            t = 144 + c
            sums = acc_s[:, 128 * c:128 * c + 128]
            if which == 0:
                parts[t // 5, t % 5] = sums
            else:
                first = lax.broadcasted_iota(jnp.int32, (8, 128), 0) == 0
                parts[t // 5, t % 5] = jnp.where(first, parts[t // 5, t % 5], sums)
    for t in range(150, 160):
        parts[t // 5, t % 5] = jnp.zeros((8, 128), F32)

    def in_plane(p):
        return (p // 8) * 16 + z_hi * 8 + p % 8

    def wait_all(ref, count, slot):
        view = ref.at[pl.ds(0, count)]
        pltpu.make_async_remote_copy(
            src_ref=view, dst_ref=view, send_sem=ssem.at[slot], recv_sem=rsem.at[slot],
            device_id=(dp, me), device_id_type=MESH,
        ).wait()

    plane[p1] = parts[p1]

    def scatter(o, carry):
        p = (p1 + o) % 32
        pltpu.make_async_remote_copy(
            src_ref=parts.at[p], dst_ref=plane.at[p1], send_sem=ssem.at[3], recv_sem=rsem.at[3],
            device_id=(dp, in_plane(p)), device_id_type=MESH,
        ).start()
        return carry

    lax.fori_loop(1, 32, scatter, 0)
    wait_all(plane, 31, 3)
    chunk[...] = plane[0]

    def add_plane(p, carry):
        chunk[...] += plane[p]
        return carry

    lax.fori_loop(1, 32, add_plane, 0)
    column[zi] = chunk[...]

    def along_z(o, carry):
        z = (zi + o) % 8
        pltpu.make_async_remote_copy(
            src_ref=chunk, dst_ref=column.at[zi], send_sem=ssem.at[4], recv_sem=rsem.at[4],
            device_id=(z % 4, x * 16 + (z // 4) * 8 + low), device_id_type=MESH,
        ).start()
        return carry

    lax.fori_loop(1, 8, along_z, 0)
    wait_all(column, 7, 4)
    total = column[0]
    for z in range(1, 8):
        total = total + column[z]
    result[...] = total * norm
    gathered[p1] = result[...]

    def gather(o, carry):
        p = (p1 + o) % 32
        pltpu.make_async_remote_copy(
            src_ref=result, dst_ref=gathered.at[p1], send_sem=ssem.at[5], recv_sem=rsem.at[5],
            device_id=(dp, in_plane(p)), device_id_type=MESH,
        ).start()
        return carry

    lax.fori_loop(1, 32, gather, 0)
    wait_all(gathered, 31, 5)
    grads_out[...] = gathered[...]

    own.wait()
    arrived(rows_out, 2)
    for slot in range(3):
        view = recv_c.at[pl.ds(0, 63 * 48)]
        pltpu.make_async_remote_copy(
            src_ref=view, dst_ref=view, send_sem=ssem.at[slot], recv_sem=rsem.at[slot],
            device_id=(dp, me), device_id_type=MESH,
        ).wait_send()


def last_kernel(factor, rows_ref, cot_ref, table_ref, grads_ref, out_ref, w1_out, b1_out, w2_out, b2_out):
    rows = rows_ref[:, 0].astype(F32)
    for half in range(2):
        image = rows[:, 8 * half:8 * half + 8, :].reshape(512, 384).astype(BF)
        for m in range(3):
            part = slice(256 * m, 256 * m + 256)
            field = dot(table_ref[part, :], image) * factor
            out_ref[half, part, :] = (cot_ref[half, part, :].astype(F32) + field).astype(BF)

    @pl.when(pl.program_id(0) == 0)
    def _():
        def tiles(first):
            return jnp.concatenate(
                [grads_ref[t // 5, t % 5] for t in range(first, first + 6)], axis=1
            )

        for which, out in enumerate((w1_out, w2_out)):
            for r in range(12):
                line = tiles(which * 72 + r * 6)
                for q in range(2):
                    for b in range(4):
                        start = q * 384 + b * 96
                        out[q, b, 8 * r:8 * r + 8, :] = line[:, start:start + 96]
        line = tiles(144)
        for which, out in enumerate((b1_out, b2_out)):
            for q in range(2):
                out[q:q + 1, :] = line[which:which + 1, 384 * q:384 * q + 384]


def local(inputs, cotangent, masks, w_first, b_first, w_second):
    factor = 1.0 / math.sqrt(384 * 768)
    norm = 1.0 / math.sqrt(4 * 256 * 256)
    lon, lon_t = lon_tables(256, 768, 64)
    lat_f, lat_b = lat_tables(256, 384)
    perm_f, perm_b = permutation(32, 4)
    cot = cotangent[0]
    any_spec = pl.BlockSpec(memory_space=pl.ANY)
    vmem = pl.BlockSpec(memory_space=pltpu.VMEM)
    wide = (1024, 768)
    rows, grads = pl.pallas_call(
        functools.partial(main_kernel, factor, norm),
        out_shape=(
            jax.ShapeDtypeStruct((3072, 384), BF),
            jax.ShapeDtypeStruct((32, 5, 8, 128), F32),
        ),
        in_specs=[any_spec] * 6 + [vmem] * 5,
        out_specs=(any_spec, vmem),
        scratch_shapes=[
            pltpu.VMEM((6, 768, 384), BF), pltpu.VMEM((6, 768, 384), BF),
            pltpu.VMEM((256, 4, 384), jnp.int32),
            pltpu.VMEM((512, 768), BF), pltpu.VMEM((512, 768), BF), pltpu.VMEM((768, 512), BF),
            pltpu.VMEM((3, 64, 16, 384), BF), pltpu.VMEM((3, 64, 16, 384), BF), pltpu.VMEM((3072, 384), BF),
            pltpu.VMEM((3072, 384), BF), pltpu.VMEM((3072, 384), BF),
            pltpu.VMEM((4, 768, 384), BF),
            pltpu.VMEM(wide, BF), pltpu.VMEM(wide, BF), pltpu.VMEM(wide, BF), pltpu.VMEM(wide, BF),
            pltpu.VMEM((4, 512, 384), BF),
            pltpu.VMEM(wide, BF), pltpu.VMEM(wide, BF),
            pltpu.VMEM((768, 768), BF), pltpu.VMEM((768, 768), BF), pltpu.VMEM((768, 768), BF),
            pltpu.VMEM((384, 768), F32), pltpu.VMEM((384, 768), F32), pltpu.VMEM((8, 768), F32),
            pltpu.VMEM((96, 768), F32),
            pltpu.VMEM((32, 5, 8, 128), F32), pltpu.VMEM((32, 5, 8, 128), F32), pltpu.VMEM((32, 5, 8, 128), F32),
            pltpu.VMEM((8, 5, 8, 128), F32), pltpu.VMEM((5, 8, 128), F32), pltpu.VMEM((5, 8, 128), F32),
            pltpu.SemaphoreType.DMA((8,)), pltpu.SemaphoreType.DMA((6,)), pltpu.SemaphoreType.DMA((6,)),
        ],
        compiler_params=pltpu.CompilerParams(
            collective_id=0, has_side_effects=True, vmem_limit_bytes=58 * MIB
        ),
        name="exchange",
    )(cot, inputs[0], masks[0], lon, lat_f, lat_b, perm_f, perm_b, w_first, b_first, w_second)
    whole = lambda shape: pl.BlockSpec(shape, lambda i: (0,) * len(shape))
    field, w1, b1, w2, b2 = pl.pallas_call(
        functools.partial(last_kernel, factor),
        out_shape=(
            jax.ShapeDtypeStruct((6, 768, 384), BF),
            jax.ShapeDtypeStruct((2, 4, 96, 96), F32),
            jax.ShapeDtypeStruct((2, 384), F32),
            jax.ShapeDtypeStruct((2, 4, 96, 96), F32),
            jax.ShapeDtypeStruct((2, 384), F32),
        ),
        grid=(3,),
        in_specs=[
            pl.BlockSpec((64, 1, 16, 384), lambda i: (0, i, 0, 0)),
            pl.BlockSpec((2, 768, 384), lambda i: (i, 0, 0)),
            whole((768, 512)),
            whole((32, 5, 8, 128)),
        ],
        out_specs=(
            pl.BlockSpec((2, 768, 384), lambda i: (i, 0, 0)),
            whole((2, 4, 96, 96)), whole((2, 384)), whole((2, 4, 96, 96)), whole((2, 384)),
        ),
        compiler_params=pltpu.CompilerParams(vmem_limit_bytes=48 * MIB),
        name="field",
    )(rows.reshape(64, 3, 16, 384), cot, lon_t, grads)
    return field[None], w1, b1, w2, b2


def solution(mesh):
    placed = (
        P("dp", "sp", None, None),
        P("dp", "sp", None, None),
        P("dp", None, "sp", None),
        P(),
        P(),
        P(),
    )
    return jax.shard_map(
        local,
        mesh=mesh,
        in_specs=placed,
        out_specs=(P("dp", "sp", None, None), P(), P(), P(), P()),
        check_vma=False,
    )
```

time: 490 us -> 209 us (0.43); the launches traced: 482 us -> 209 us
  waiting for transfers between devices: 218 us -> 0 us
  Pallas kernels: 0 us -> 205 us
  blocking collectives: 99 us -> 0 us
  local copies, waits for them, and re-layouts: 53.3 us -> 2.75 us
  starting transfers between devices: 35.3 us -> 0 us
  matrix products: 32.6 us -> 0 us
  other arithmetic: 29.1 us -> 0 us
  between operations: 15 us -> 0.7 us
    pallas_call x0 -> x2, Pallas kernels: none -> 205 us  [the longest x1 199 us: local(): pl.pallas_call(functools.partial(main_kernel, factor, norm), out_shape=(j...]
    psum x1 -> x0, waiting for transfers between devices: 173 us -> none  [local(): lax.psum((first_terms[0], first_terms[1], second_terms[0], second_terms[1...]
    psum x1 -> x0, blocking collectives: 99 us -> none  [local(): lax.psum((first_terms[0], first_terms[1], second_terms[0], second_terms[1...]
    all_to_all x3 -> x0, waiting for transfers between devices: 45 us -> none  [the longest x1 45 us: local(): lax.all_to_all(y_cotan, 'sp', split_axis=1, concat_axis=2, tiled=True)]
    all_to_all x3 -> x0, starting transfers between devices: 35 us -> none  [the longest x1 16.5 us: local(): lax.all_to_all(y_cotan, 'sp', split_axis=1, concat_axis=2, tiled=True)]
    dot_general x26 -> x0, matrix products: 32.6 us -> none  [contract(): return jnp.einsum(form, left, right, preferred_element_type=jnp.float32)]
    unnamed x49 -> x6, local copies, waits for them, and re-layouts: 18.4 us -> 2.75 us
    convert_element_type x5 -> x0, local copies, waits for them, and re-layouts: 15.6 us -> none  [the longest x2 7.69 us: row_spectrum(): return contract('pkw,hwc->pkhc', lon_tab, field[0]).astype(jnp.bfloat16)]
  transfers between devices with their start and end apart: 4 -> 0, of which waited for: 2 -> 0; matrix products, arithmetic and copies ran while one was open for 14% -> 0% of each run, Pallas kernels for 0% -> 0%
where the time goes in v1:
time: 209 us
  Pallas kernels  205 us (98%)
  local copies, waits for them, and re-layouts  2.75 us (1%)
    pallas_call x1, Pallas kernels, local(): pl.pallas_call(functools.partial(main_kernel, factor, norm), out_shape=(j...  199 us
    pallas_call x1, Pallas kernels, local(): pl.pallas_call(functools.partial(last_kernel, factor), out_shape=(jax.Sha...  6.6 us

profile of v1, /device:TPU:1, one launch (start us, length us, event | category | flops | bytes accessed | tf_op | source)
XLA Modules:
  0.0 208.8 jit_solution(5561842891705572142)
XLA Ops:
  0.6 0.0 copy-start.1
  0.6 198.7 %exchange.1 = (bf16[3072,384]{1,0:T(8,128)(2,1)}, f32[32,5,8,128]{3,2,1,0:T(8,128)}) custom-call(bf16[6,768,384]{2,1,0:T(8,128)(2,1)} %bitcast.6, bf16[6,768,384]{2,1,0:T(8,128)(2,1)} %bitcast.8, s32[256,4,384]{2,1,0:T(4,128)} %bitcast.9, bf16[512,768]{1,0:T(8,128)(2,1)} %constant.12.clone.lon_hbm, bf16[512,768]{1,0:T(8,128)(2,1)} %constant.13.clone.latf_hbm, ...), custom_call_target="tpu_custom_call" | custom-call | tf_op jit(solution)/shard_map/exchange/pallas_call | solution.py:411
  199.4 0.0 copy-done.1
  199.4 0.0 copy-start
  199.4 1.7 copy-done
  201.1 0.0 copy-start.2
  201.1 1.1 copy-done.2
  202.2 6.6 %field.1 = (bf16[6,768,384]{2,1,0:T(8,128)(2,1)}, f32[2,4,96,96]{3,2,1,0:T(8,128)}, f32[2,384]{1,0:T(2,128)}, f32[2,4,96,96]{3,2,1,0:T(8,128)}, f32[2,384]{1,0:T(2,128)}) custom-call(bf16[64,3,16,384]{3,2,1,0:T(8,128)(2,1)S(1)} %bitcast.5, bf16[6,768,384]{2,1,0:T(8,128)(2,1)} %bitcast.7, bf16[768,512]{1,0:T(8,128)(2,1)S(1)} %copy-done.1, ...), custom_call_target="tpu_custom_call" | custom-call | tf_op jit(solution)/shard_map/field/pallas_call | solution.py:442
Async XLA Ops:
  0.6 198.8 %copy-start.1 = (bf16[768,512]{1,0:T(8,128)(2,1)S(1)}, bf16[768,512]{1,0:T(8,128)(2,1)}, u32[]{:S(2)}) copy-start(bf16[768,512]{1,0:T(8,128)(2,1)} %constant.17.clone.table_ref) | copy-start | bytes 2359300
  199.4 1.7 copy-start
  201.1 1.1 copy-start.2

commit v2 on v1

--- a/solution.py
+++ b/solution.py
@@ -14,6 +14,7 @@
 BF = jnp.bfloat16
 F32 = jnp.float32
 MIB = 2**20
+AHEAD = 24
 
 
 def bf(array):
@@ -34,7 +35,9 @@
     angle = (np.float32(2.0 * math.pi / length) * phase.astype(np.float32)).astype(np.float64)
     cosine, sine = np.cos(angle), np.sin(angle)
     forward = np.stack([np.stack([cosine, sine], 2), np.stack([-sine, cosine], 2)])
-    return bf(forward.reshape(2 * keep, 2 * length)), bf(forward.reshape(2 * keep, 2 * length).T)
+    forward = forward.reshape(2 * keep, 2 * length)
+    backward = forward.T.reshape(4, 2, 8, 12, 2 * keep).transpose(1, 0, 2, 3, 4)
+    return bf(forward), bf(backward.reshape(2 * length, 2 * keep))
 
 
 def permutation(rows, modes):
@@ -58,10 +61,10 @@
 
 def main_kernel(
     factor, norm,
-    cot_hbm, inp_hbm, mask_hbm, lon_hbm, latf_hbm, latb_hbm, pf_ref, pb_ref, w1_ref, b1_ref, w2_ref,
+    cot_hbm, inp_hbm, mask_hbm, lon_hbm, latf_hbm, latb_hbm, pf_hbm, pb_hbm, w1_hbm, b1_hbm, w2_hbm,
     rows_out, grads_out,
-    cot_v, inp_v, mask_v, lon_v, latf_v, latb_v,
-    send_c, send_i, send_r, recv_c, recv_i, xt, spec, dtwo, done, hid, dsp, relu, shrink,
+    cot_v, inp_v, mask_v, lon_v, latf_v, latb_v, pf_ref, pb_ref, w1_ref, b1_ref, w2_ref,
+    send_c, send_i, send_r, relay, recv_c, recv_i, xt, spec, dtwo, done, hid, dsp, relu, shrink,
     m1, m2, m3, acc_a, acc_b, acc_s, fold, parts, gathered, plane, column, chunk, result,
     lsem, ssem, rsem,
 ):
@@ -74,13 +77,17 @@
     zi = z_hi * 4 + dp
 
     loads = [
-        pltpu.make_async_copy(lon_hbm, lon_v, lsem.at[0]),
-        pltpu.make_async_copy(cot_hbm.at[pl.ds(0, 2)], cot_v.at[pl.ds(0, 2)], lsem.at[1]),
-        pltpu.make_async_copy(cot_hbm.at[pl.ds(2, 4)], cot_v.at[pl.ds(2, 4)], lsem.at[2]),
-        pltpu.make_async_copy(inp_hbm, inp_v, lsem.at[3]),
-        pltpu.make_async_copy(mask_hbm, mask_v, lsem.at[4]),
-        pltpu.make_async_copy(latf_hbm, latf_v, lsem.at[5]),
-        pltpu.make_async_copy(latb_hbm, latb_v, lsem.at[6]),
+        pltpu.make_async_copy(there, here, lsem.at[i])
+        for i, (there, here) in enumerate((
+            (lon_hbm.at[pl.ds(0, 256)], lon_v.at[pl.ds(0, 256)]),
+            (cot_hbm.at[0], cot_v.at[0]),
+            (cot_hbm.at[1], cot_v.at[1]),
+            (lon_hbm.at[pl.ds(256, 256)], lon_v.at[pl.ds(256, 256)]),
+            (cot_hbm.at[pl.ds(2, 4)], cot_v.at[pl.ds(2, 4)]),
+            (inp_hbm, inp_v),
+            (w1_hbm, w1_ref), (w2_hbm, w2_ref), (b1_hbm, b1_ref),
+            (mask_hbm, mask_v), (latf_hbm, latf_v), (latb_hbm, latb_v), (pf_hbm, pf_ref), (pb_hbm, pb_ref),
+        ))
     ]
     for load in loads:
         load.start()
@@ -122,12 +129,12 @@
 
         lax.fori_loop(1, 64, one, 0)
 
-    loads[0].wait()
-    loads[1].wait()
+    for load in loads[:4]:
+        load.wait()
     transform(cot_v, send_c, 0)
     pl.semaphore_wait(barrier, 69)
     send_rows(send_c, recv_c, 0, 0)
-    loads[2].wait()
+    loads[4].wait()
 
     def cot_pair(hp, carry):
         transform(cot_v, send_c, hp)
@@ -135,7 +142,7 @@
         return carry
 
     lax.fori_loop(1, 3, cot_pair, 0)
-    loads[3].wait()
+    loads[5].wait()
 
     def inp_pair(hp, carry):
         transform(inp_v, send_i, hp)
@@ -143,6 +150,9 @@
         return carry
 
     lax.fori_loop(0, 3, inp_pair, 0)
+
+    for load in loads[6:]:
+        load.wait()
 
     lane = lax.broadcasted_iota(jnp.int32, (96, 384), 1)
     row = lax.broadcasted_iota(jnp.int32, (96, 384), 0)
@@ -163,7 +173,6 @@
             target[up, 384:768] = -imag
             target[dn, 0:384] = imag
             target[dn, 384:768] = real
-    loads[4].wait()
     for kk in range(4):
         bits = mask_v[:, kk, :]
         here = slice(256 * kk, 256 * kk + 256)
@@ -171,8 +180,6 @@
         relu[here, 384:768] = ((bits >> 1) & 1).astype(F32).astype(BF)
         shrink[here, 0:384] = ((bits >> 2) & 1).astype(F32).astype(BF)
         shrink[here, 384:768] = ((bits >> 3) & 1).astype(F32).astype(BF)
-    loads[5].wait()
-    loads[6].wait()
 
     def arrived(recv, slot):
         view = recv.at[pl.ds(0, 63 * 48)]
@@ -212,11 +219,6 @@
 
     lax.fori_loop(0, 4, adjoint, 0)
 
-    own = pltpu.make_async_copy(
-        send_r.at[pl.ds(pl.multiple_of(me * 48, 16), 48)],
-        rows_out.at[pl.ds(pl.multiple_of(me * 48, 16), 48)], lsem.at[7],
-    )
-
     def image_quarter(m):
         def block(b, carry):
             table = latb_v[pl.ds(pl.multiple_of(m * 192 + b * 64, 64), 64), :]
@@ -227,25 +229,55 @@
 
         lax.fori_loop(0, 3, block, 0)
 
-    for i in range(4):
-        m = (x + i) % 4
-        image_quarter(m)
-        if i == 0:
-            own.start()
-
+    def rows48(index):
+        return pl.ds(pl.multiple_of(index * 48, 16), 48)
+
+    def in_plane(p):
+        return (p // 8) * 16 + z_hi * 8 + p % 8
+
+    other = me + 8 - 16 * z_hi
+    mine = z_hi * 32
+    theirs = 32 - mine
+
+    def send_in_plane(base, target, slot):
         def one(o, carry):
-            there = m * 16 + (me + o) % 16
+            p = (p1 + o) % 32
             pltpu.make_async_remote_copy(
-                src_ref=send_r.at[pl.ds(pl.multiple_of(there * 48, 16), 48)],
-                dst_ref=rows_out.at[pl.ds(pl.multiple_of(me * 48, 16), 48)],
-                send_sem=ssem.at[2], recv_sem=rsem.at[2],
-                device_id=(dp, there), device_id_type=MESH,
+                src_ref=send_r.at[rows48(base + p)], dst_ref=target, send_sem=ssem.at[6],
+                recv_sem=rsem.at[slot], device_id=(dp, in_plane(p)), device_id_type=MESH,
             ).start()
             return carry
 
-        lax.fori_loop(1 if i == 0 else 0, 16, one, 0)
+        lax.fori_loop(1, 32, one, 0)
+
+    def send_across(first, last):
+        def one(p, carry):
+            pltpu.make_async_remote_copy(
+                src_ref=relay.at[rows48(p)], dst_ref=rows_out.at[rows48(in_plane(p))],
+                send_sem=ssem.at[7], recv_sem=rsem.at[2],
+                device_id=(dp, other), device_id_type=MESH,
+            ).start()
+            return carry
+
+        lax.fori_loop(first, last, one, 0)
+
+    image_quarter(theirs // 16)
+    image_quarter(theirs // 16 + 1)
+    send_in_plane(theirs, relay.at[rows48(p1)], 6)
+    relay[rows48(p1), :] = send_r[rows48(theirs + p1), :]
+    image_quarter(mine // 16)
+    image_quarter(mine // 16 + 1)
+    own = pltpu.make_async_copy(send_r.at[rows48(mine + p1)], rows_out.at[rows48(me)], lsem.at[14])
+    own.start()
+    send_in_plane(mine, rows_out.at[rows48(me)], 2)
 
     arrived(recv_i, 1)
+    view = relay.at[pl.ds(0, 31 * 48)]
+    pltpu.make_async_remote_copy(
+        src_ref=view, dst_ref=view, send_sem=ssem.at[6], recv_sem=rsem.at[6],
+        device_id=(dp, me), device_id_type=MESH,
+    ).wait_recv()
+    send_across(0, AHEAD)
     by_mode(recv_i)
 
     def layer(kk, carry):
@@ -300,9 +332,6 @@
     for t in range(150, 160):
         parts[t // 5, t % 5] = jnp.zeros((8, 128), F32)
 
-    def in_plane(p):
-        return (p // 8) * 16 + z_hi * 8 + p % 8
-
     def wait_all(ref, count, slot):
         view = ref.at[pl.ds(0, count)]
         pltpu.make_async_remote_copy(
@@ -340,6 +369,7 @@
         return carry
 
     lax.fori_loop(1, 8, along_z, 0)
+    send_across(AHEAD, 32)
     wait_all(column, 7, 4)
     total = column[0]
     for z in range(1, 8):
@@ -357,45 +387,120 @@
 
     lax.fori_loop(1, 32, gather, 0)
     wait_all(gathered, 31, 5)
-    grads_out[...] = gathered[...]
-
+    grads = pltpu.make_async_copy(gathered, grads_out, lsem.at[15])
+    grads.start()
+
+    grads.wait()
     own.wait()
     arrived(rows_out, 2)
-    for slot in range(3):
-        view = recv_c.at[pl.ds(0, 63 * 48)]
+    for slot, count in ((0, 63), (1, 63), (6, 62), (7, 32)):
+        view = recv_c.at[pl.ds(0, count * 48)]
         pltpu.make_async_remote_copy(
             src_ref=view, dst_ref=view, send_sem=ssem.at[slot], recv_sem=rsem.at[slot],
             device_id=(dp, me), device_id_type=MESH,
         ).wait_send()
 
 
-def last_kernel(factor, rows_ref, cot_ref, table_ref, grads_ref, out_ref, w1_out, b1_out, w2_out, b2_out):
-    rows = rows_ref[:, 0].astype(F32)
-    for half in range(2):
-        image = rows[:, 8 * half:8 * half + 8, :].reshape(512, 384).astype(BF)
+def last_kernel(
+    factor, rows_hbm, cot_hbm, table_hbm, grads_hbm, out_hbm, w1_hbm, b1_hbm, w2_hbm, b2_hbm,
+    rows_v, cot_v, table_v, grads_v, out_v, w1_v, b1_v, w2_v, b2_v, rsem, csem, tsem, osem, gsem,
+):
+    table_load = [
+        pltpu.make_async_copy(table_hbm.at[pl.ds(256 * m, 256)], table_v.at[pl.ds(256 * m, 256)], tsem.at[m])
+        for m in range(3)
+    ]
+    rows_load = [
+        [
+            pltpu.make_async_copy(
+                rows_hbm.at[pl.ds(32 * s, 32), hp], rows_v.at[hp, pl.ds(32 * s, 32)], rsem.at[hp, s]
+            )
+            for s in range(2)
+        ]
+        for hp in range(3)
+    ]
+    cot_load = [pltpu.make_async_copy(cot_hbm.at[h], cot_v.at[h], csem.at[h]) for h in range(6)]
+    grads_load = pltpu.make_async_copy(grads_hbm, grads_v, gsem.at[0])
+    for load in rows_load[0]:
+        load.start()
+    for load in table_load:
+        load.start()
+    for hp in range(3):
+        cot_load[2 * hp].start()
+        cot_load[2 * hp + 1].start()
+        if hp == 0:
+            grads_load.start()
+        if hp < 2:
+            for load in rows_load[hp + 1]:
+                load.start()
+
+    stores = [pltpu.make_async_copy(out_v.at[h], out_hbm.at[h], osem.at[h]) for h in range(6)]
+    small = [
+        pltpu.make_async_copy(here, there, gsem.at[1 + i])
+        for i, (here, there) in enumerate(((w1_v, w1_hbm), (b1_v, b1_hbm), (w2_v, w2_hbm), (b2_v, b2_hbm)))
+    ]
+
+    def tiles(first):
+        return jnp.concatenate([grads_v[t // 5, t % 5] for t in range(first, first + 6)], axis=1)
+
+    for hp in range(3):
+        for load in rows_load[hp]:
+            load.wait()
+        rows = rows_v[hp].astype(F32)
+        for half in range(2):
+            image = rows[:, 8 * half:8 * half + 8, :].reshape(512, 384).astype(BF)
+            if half == 0:
+                first = image
+        for h in (2 * hp, 2 * hp + 1):
+            cot_load[h].wait()
+        pair = jnp.concatenate([first, image], axis=1)
         for m in range(3):
+            if hp == 0:
+                table_load[m].wait()
             part = slice(256 * m, 256 * m + 256)
-            field = dot(table_ref[part, :], image) * factor
-            out_ref[half, part, :] = (cot_ref[half, part, :].astype(F32) + field).astype(BF)
-
-    @pl.when(pl.program_id(0) == 0)
-    def _():
-        def tiles(first):
-            return jnp.concatenate(
-                [grads_ref[t // 5, t % 5] for t in range(first, first + 6)], axis=1
-            )
-
-        for which, out in enumerate((w1_out, w2_out)):
-            for r in range(12):
-                line = tiles(which * 72 + r * 6)
+            field = dot(table_v[part, :], pair) * factor
+            for half in range(2):
+                h = 2 * hp + half
+                cols = slice(384 * half, 384 * half + 384)
+                out_v[h, part, :] = (cot_v[h, part, :].astype(F32) + field[:, cols]).astype(BF)
+        for h in (2 * hp, 2 * hp + 1):
+            stores[h].start()
+        if hp == 0:
+            grads_load.wait()
+            for which, out in enumerate((w1_v, w2_v)):
+                for r in range(12):
+                    line = tiles(which * 72 + r * 6)
+                    for q in range(2):
+                        for b in range(4):
+                            start = q * 384 + b * 96
+                            out[q, b, 8 * r:8 * r + 8, :] = line[:, start:start + 96]
+            line = tiles(144)
+            for which, out in enumerate((b1_v, b2_v)):
                 for q in range(2):
-                    for b in range(4):
-                        start = q * 384 + b * 96
-                        out[q, b, 8 * r:8 * r + 8, :] = line[:, start:start + 96]
-        line = tiles(144)
-        for which, out in enumerate((b1_out, b2_out)):
-            for q in range(2):
-                out[q:q + 1, :] = line[which:which + 1, 384 * q:384 * q + 384]
+                    out[q:q + 1, :] = line[which:which + 1, 384 * q:384 * q + 384]
+            for copy in small:
+                copy.start()
+    for copy in small + stores:
+        copy.wait()
+
+
+def last_call(factor, rows, cot, table, grads):
+    any_spec = pl.BlockSpec(memory_space=pl.ANY)
+    small = [(2, 4, 96, 96), (2, 384)] * 2
+    return pl.pallas_call(
+        functools.partial(last_kernel, factor),
+        out_shape=(jax.ShapeDtypeStruct((6, 768, 384), BF),) + tuple(jax.ShapeDtypeStruct(s, F32) for s in small),
+        in_specs=[any_spec] * 4,
+        out_specs=(any_spec,) * 5,
+        scratch_shapes=[
+            pltpu.VMEM((3, 64, 16, 384), BF), pltpu.VMEM((6, 768, 384), BF), pltpu.VMEM((768, 512), BF),
+            pltpu.VMEM((32, 5, 8, 128), F32), pltpu.VMEM((6, 768, 384), BF),
+        ] + [pltpu.VMEM(s, F32) for s in small] + [
+            pltpu.SemaphoreType.DMA((3, 2)), pltpu.SemaphoreType.DMA((6,)), pltpu.SemaphoreType.DMA((3,)),
+            pltpu.SemaphoreType.DMA((6,)), pltpu.SemaphoreType.DMA((5,)),
+        ],
+        compiler_params=pltpu.CompilerParams(vmem_limit_bytes=62 * MIB),
+        name="field",
+    )(rows, cot, table, grads)
 
 
 def local(inputs, cotangent, masks, w_first, b_first, w_second):
@@ -406,7 +511,6 @@
     perm_f, perm_b = permutation(32, 4)
     cot = cotangent[0]
     any_spec = pl.BlockSpec(memory_space=pl.ANY)
-    vmem = pl.BlockSpec(memory_space=pltpu.VMEM)
     wide = (1024, 768)
     rows, grads = pl.pallas_call(
         functools.partial(main_kernel, factor, norm),
@@ -414,13 +518,15 @@
             jax.ShapeDtypeStruct((3072, 384), BF),
             jax.ShapeDtypeStruct((32, 5, 8, 128), F32),
         ),
-        in_specs=[any_spec] * 6 + [vmem] * 5,
-        out_specs=(any_spec, vmem),
+        in_specs=[any_spec] * 11,
+        out_specs=(any_spec, any_spec),
         scratch_shapes=[
             pltpu.VMEM((6, 768, 384), BF), pltpu.VMEM((6, 768, 384), BF),
             pltpu.VMEM((256, 4, 384), jnp.int32),
             pltpu.VMEM((512, 768), BF), pltpu.VMEM((512, 768), BF), pltpu.VMEM((768, 512), BF),
-            pltpu.VMEM((3, 64, 16, 384), BF), pltpu.VMEM((3, 64, 16, 384), BF), pltpu.VMEM((3072, 384), BF),
+            pltpu.VMEM((256, 256), BF), pltpu.VMEM((256, 256), BF),
+            pltpu.VMEM((2, 4, 96, 96), BF), pltpu.VMEM((2, 384), F32), pltpu.VMEM((2, 4, 96, 96), BF),
+            pltpu.VMEM((3, 64, 16, 384), BF), pltpu.VMEM((3, 64, 16, 384), BF), pltpu.VMEM((3072, 384), BF), pltpu.VMEM((1536, 384), BF),
             pltpu.VMEM((3072, 384), BF), pltpu.VMEM((3072, 384), BF),
             pltpu.VMEM((4, 768, 384), BF),
             pltpu.VMEM(wide, BF), pltpu.VMEM(wide, BF), pltpu.VMEM(wide, BF), pltpu.VMEM(wide, BF),
@@ -431,37 +537,14 @@
             pltpu.VMEM((96, 768), F32),
             pltpu.VMEM((32, 5, 8, 128), F32), pltpu.VMEM((32, 5, 8, 128), F32), pltpu.VMEM((32, 5, 8, 128), F32),
             pltpu.VMEM((8, 5, 8, 128), F32), pltpu.VMEM((5, 8, 128), F32), pltpu.VMEM((5, 8, 128), F32),
-            pltpu.SemaphoreType.DMA((8,)), pltpu.SemaphoreType.DMA((6,)), pltpu.SemaphoreType.DMA((6,)),
+            pltpu.SemaphoreType.DMA((16,)), pltpu.SemaphoreType.DMA((8,)), pltpu.SemaphoreType.DMA((7,)),
         ],
         compiler_params=pltpu.CompilerParams(
-            collective_id=0, has_side_effects=True, vmem_limit_bytes=58 * MIB
+            collective_id=0, has_side_effects=True, vmem_limit_bytes=62 * MIB
         ),
         name="exchange",
     )(cot, inputs[0], masks[0], lon, lat_f, lat_b, perm_f, perm_b, w_first, b_first, w_second)
-    whole = lambda shape: pl.BlockSpec(shape, lambda i: (0,) * len(shape))
-    field, w1, b1, w2, b2 = pl.pallas_call(
-        functools.partial(last_kernel, factor),
-        out_shape=(
-            jax.ShapeDtypeStruct((6, 768, 384), BF),
-            jax.ShapeDtypeStruct((2, 4, 96, 96), F32),
-            jax.ShapeDtypeStruct((2, 384), F32),
-            jax.ShapeDtypeStruct((2, 4, 96, 96), F32),
-            jax.ShapeDtypeStruct((2, 384), F32),
-        ),
-        grid=(3,),
-        in_specs=[
-            pl.BlockSpec((64, 1, 16, 384), lambda i: (0, i, 0, 0)),
-            pl.BlockSpec((2, 768, 384), lambda i: (i, 0, 0)),
-            whole((768, 512)),
-            whole((32, 5, 8, 128)),
-        ],
-        out_specs=(
-            pl.BlockSpec((2, 768, 384), lambda i: (i, 0, 0)),
-            whole((2, 4, 96, 96)), whole((2, 384)), whole((2, 4, 96, 96)), whole((2, 384)),
-        ),
-        compiler_params=pltpu.CompilerParams(vmem_limit_bytes=48 * MIB),
-        name="field",
-    )(rows.reshape(64, 3, 16, 384), cot, lon_t, grads)
+    field, w1, b1, w2, b2 = last_call(factor, rows.reshape(64, 3, 16, 384), cot, lon_t, grads)
     return field[None], w1, b1, w2, b2
 
 

time: 209 us -> 194 us (0.928)
  Pallas kernels: 205 us -> 192 us
  local copies, waits for them, and re-layouts: 2.75 us -> 0 us
    pallas_call x1, Pallas kernels: 199 us -> 186 us  [local(): pl.pallas_call(functools.partial(main_kernel, factor, norm), out_shape=(j...]
    unnamed x6 -> x0, local copies, waits for them, and re-layouts: 2.75 us -> none
where the time goes in v2:
time: 194 us; the launch traced here: 193 us
  Pallas kernels  192 us (99%)
    pallas_call x1, Pallas kernels, local(): pl.pallas_call(functools.partial(main_kernel, factor, norm), out_shape=(j...  186 us
    pallas_call x1, Pallas kernels, last_call(): pl.pallas_call(functools.partial(last_kernel, factor), out_shape=(jax.Sha...  6.48 us

profile of v2, /device:TPU:1, one launch (start us, length us, event | category | flops | bytes accessed | tf_op | source)
XLA Modules:
  0.0 192.8 jit_solution(17370639365236950723)
XLA Ops:
  0.6 185.5 %exchange.1 = (bf16[3072,384]{1,0:T(8,128)(2,1)}, f32[32,5,8,128]{3,2,1,0:T(8,128)}) custom-call(bf16[6,768,384]{2,1,0:T(8,128)(2,1)} %bitcast.5, bf16[6,768,384]{2,1,0:T(8,128)(2,1)} %bitcast.7, s32[256,4,384]{2,1,0:T(4,128)} %bitcast.9, bf16[512,768]{1,0:T(8,128)(2,1)} %constant.12.clone.lon_hbm, bf16[512,768]{1,0:T(8,128)(2,1)} %constant.13.clone.latf_hbm, ...), custom_call_target="tpu_custom_call" | custom-call | tf_op jit(solution)/shard_map/exchange/pallas_call | solution.py:515
  186.2 6.5 %field.1 = (bf16[6,768,384]{2,1,0:T(8,128)(2,1)}, f32[2,4,96,96]{3,2,1,0:T(8,128)}, f32[2,384]{1,0:T(2,128)}, f32[2,4,96,96]{3,2,1,0:T(8,128)}, f32[2,384]{1,0:T(2,128)}) custom-call(bf16[64,3,16,384]{3,2,1,0:T(8,128)(2,1)} %bitcast.8, bf16[6,768,384]{2,1,0:T(8,128)(2,1)} %bitcast.6, bf16[768,512]{1,0:T(8,128)(2,1)} %constant.17.clone.table_hbm, ...), custom_call_target="tpu_custom_call" | custom-call | tf_op jit(solution)/shard_map/field/pallas_call | solution.py:489

commit v3 on v2

--- a/solution.py
+++ b/solution.py
@@ -14,7 +14,8 @@
 BF = jnp.bfloat16
 F32 = jnp.float32
 MIB = 2**20
-AHEAD = 24
+AHEAD = 20
+DIRECT = 8
 
 
 def bf(array):
@@ -239,7 +240,7 @@
     mine = z_hi * 32
     theirs = 32 - mine
 
-    def send_in_plane(base, target, slot):
+    def send_in_plane(base, target, slot, first):
         def one(o, carry):
             p = (p1 + o) % 32
             pltpu.make_async_remote_copy(
@@ -248,10 +249,19 @@
             ).start()
             return carry
 
-        lax.fori_loop(1, 32, one, 0)
+        lax.fori_loop(first, 32, one, 0)
+
+    def send_direct(o, carry):
+        p = (p1 + o) % 32
+        pltpu.make_async_remote_copy(
+            src_ref=send_r.at[rows48(theirs + p)], dst_ref=rows_out.at[rows48(me)], send_sem=ssem.at[6],
+            recv_sem=rsem.at[2], device_id=(dp, in_plane(p) + 8 - 16 * z_hi), device_id_type=MESH,
+        ).start()
+        return carry
 
     def send_across(first, last):
-        def one(p, carry):
+        def one(o, carry):
+            p = (p1 + 64 - o) % 32
             pltpu.make_async_remote_copy(
                 src_ref=relay.at[rows48(p)], dst_ref=rows_out.at[rows48(in_plane(p))],
                 send_sem=ssem.at[7], recv_sem=rsem.at[2],
@@ -259,20 +269,21 @@
             ).start()
             return carry
 
-        lax.fori_loop(first, last, one, 0)
+        lax.fori_loop(DIRECT + 1 + first, DIRECT + 1 + last, one, 0)
 
     image_quarter(theirs // 16)
     image_quarter(theirs // 16 + 1)
-    send_in_plane(theirs, relay.at[rows48(p1)], 6)
+    send_in_plane(theirs, relay.at[rows48(p1)], 6, DIRECT + 1)
+    lax.fori_loop(1, DIRECT + 1, send_direct, 0)
     relay[rows48(p1), :] = send_r[rows48(theirs + p1), :]
     image_quarter(mine // 16)
     image_quarter(mine // 16 + 1)
     own = pltpu.make_async_copy(send_r.at[rows48(mine + p1)], rows_out.at[rows48(me)], lsem.at[14])
     own.start()
-    send_in_plane(mine, rows_out.at[rows48(me)], 2)
+    send_in_plane(mine, rows_out.at[rows48(me)], 2, 1)
 
     arrived(recv_i, 1)
-    view = relay.at[pl.ds(0, 31 * 48)]
+    view = relay.at[pl.ds(0, (31 - DIRECT) * 48)]
     pltpu.make_async_remote_copy(
         src_ref=view, dst_ref=view, send_sem=ssem.at[6], recv_sem=rsem.at[6],
         device_id=(dp, me), device_id_type=MESH,
@@ -369,7 +380,7 @@
         return carry
 
     lax.fori_loop(1, 8, along_z, 0)
-    send_across(AHEAD, 32)
+    send_across(AHEAD, 32 - DIRECT)
     wait_all(column, 7, 4)
     total = column[0]
     for z in range(1, 8):
@@ -393,7 +404,7 @@
     grads.wait()
     own.wait()
     arrived(rows_out, 2)
-    for slot, count in ((0, 63), (1, 63), (6, 62), (7, 32)):
+    for slot, count in ((0, 63), (1, 63), (6, 62), (7, 32 - DIRECT)):
         view = recv_c.at[pl.ds(0, count * 48)]
         pltpu.make_async_remote_copy(
             src_ref=view, dst_ref=view, send_sem=ssem.at[slot], recv_sem=rsem.at[slot],

time: 194 us -> 192 us (0.990)
  no operation moved by 1% of the time
where the time goes in v3:
time: 192 us
  Pallas kernels  191 us (99%)
    pallas_call x1, Pallas kernels, local(): pl.pallas_call(functools.partial(main_kernel, factor, norm), out_shape=(j...  184 us
    pallas_call x1, Pallas kernels, last_call(): pl.pallas_call(functools.partial(last_kernel, factor), out_shape=(jax.Sha...  6.48 us

profile of v3, /device:TPU:1, one launch (start us, length us, event | category | flops | bytes accessed | tf_op | source)
XLA Modules:
  0.0 191.6 jit_solution(11502566530242442404)
XLA Ops:
  0.6 184.3 %exchange.1 = (bf16[3072,384]{1,0:T(8,128)(2,1)}, f32[32,5,8,128]{3,2,1,0:T(8,128)}) custom-call(bf16[6,768,384]{2,1,0:T(8,128)(2,1)} %bitcast.5, bf16[6,768,384]{2,1,0:T(8,128)(2,1)} %bitcast.7, s32[256,4,384]{2,1,0:T(4,128)} %bitcast.9, bf16[512,768]{1,0:T(8,128)(2,1)} %constant.12.clone.lon_hbm, bf16[512,768]{1,0:T(8,128)(2,1)} %constant.13.clone.latf_hbm, ...), custom_call_target="tpu_custom_call" | custom-call | tf_op jit(solution)/shard_map/exchange/pallas_call | solution.py:526
  185.0 6.5 %field.1 = (bf16[6,768,384]{2,1,0:T(8,128)(2,1)}, f32[2,4,96,96]{3,2,1,0:T(8,128)}, f32[2,384]{1,0:T(2,128)}, f32[2,4,96,96]{3,2,1,0:T(8,128)}, f32[2,384]{1,0:T(2,128)}) custom-call(bf16[64,3,16,384]{3,2,1,0:T(8,128)(2,1)} %bitcast.8, bf16[6,768,384]{2,1,0:T(8,128)(2,1)} %bitcast.6, bf16[768,512]{1,0:T(8,128)(2,1)} %constant.17.clone.table_hbm, ...), custom_call_target="tpu_custom_call" | custom-call | tf_op jit(solution)/shard_map/field/pallas_call | solution.py:500
